TPU v7x, 32 devices: a whole 2x2x4 slice. The times are simulated.
32 devices in a mesh: groups: 2 (over y), lon: 4 (over z), lat: 2 (over x), ch: 2 (over core).
Axes of the slice: x: 2, y: 2, z: 4, core: 2. Of those that a mesh axis runs over, the one named last changes fastest.
Arguments:
- features: float32 [12288, 256], P(('groups', 'lon', 'lat'), 'ch'), parts along dimension 0, may hold values from -6 to 6
- blocks: float32 [48, 3, 128, 128], P(('lon', 'lat')), may hold values from -0.3125 to 0.3125
- sources: int32 [48, 3], P(('lon', 'lat')), may hold values from 0 to 9, as said below
- live: int32 [8], P(('lon', 'lat')), may hold values from 4 to 6, as said below
- weights: float32 [4, 256, 256], P(None, None, 'ch'), may hold values from -0.1875 to 0.1875
- cotangent: float32 [12288, 256], P(('groups', 'lon', 'lat'), 'ch'), parts along dimension 0, may hold values from -6 to 6
Outputs:
- output: float32 [12288, 256], P(('groups', 'lon', 'lat'), 'ch'), parts along dimension 0
- input_grad: float32 [12288, 256], P(('groups', 'lon', 'lat'), 'ch'), parts along dimension 0
- weight_grad: float32 [8, 256, 256], P('groups', None, 'ch'), parts along dimension 0
There are 2 independent parts, one for each index of `groups`. A program takes and returns all parts, laid end to end along the dimension named above; an argument that names none is the same for every part. Nothing has to cross between parts.
Inputs may be any that keep to these rules, and one draw needn't show every extreme that they name: `sources`: on tile t of every sector and band, block 0 reads tile t itself; for t < 4, block 1 reads extended entry 6 + t; other blocks read any entry of the extended list. Bands other than the first and last are fully live; in those two, sector 0 holds 6 live tiles, sector 1 holds 4, and the others 6 - 2 to 6.
All inputs are finite; a program needn't handle non-finite values.
Results may differ from a plain program's by a relative error of at most 0.0003.
Values sent between devices are 32-bit elements; how exact they have to be, the bound alone decides.
A program may use at most 64 MiB of HBM per device.

v0:
```python
import jax
import jax.numpy as jnp
from jax import lax
from jax.sharding import PartitionSpec as P

CHEB = 4
TILE = 128
TILES = 6


highest_accuracy = lax.Precision.HIGHEST


def padded(array, sides, width, wrap):
    for axis, dim in sides:
        devices, length = (lax.axis_size(axis), array.shape[dim])
        up = [(i, (i + 1) % devices) for i in range(devices if wrap else devices - 1)]
        down = [(j, i) for i, j in up]
        last = lax.slice_in_dim(array, length - width, length, axis=dim)
        leading = lax.slice_in_dim(array, 0, width, axis=dim)
        before = lax.ppermute(last, axis, up)
        after = lax.ppermute(leading, axis, down)
        array = jnp.concatenate([before, array, after], axis=dim)
    return array


def lon_edges(paired):
    return padded(paired, (("lon", 0),), 1, True)


def lat_edges(paired):
    return padded(paired, (("lat", 0),), 1, False)


def forward_apply(pixel_field, blocks, sources, keep_mask):
    lon_padded = lon_edges(pixel_field[0:2])
    lat_padded = lat_edges(pixel_field[2:4])
    extended = jnp.concatenate(
        [pixel_field, lon_padded[0:1], lon_padded[3:4], lat_padded[0:1], lat_padded[3:4]], axis=0
    )
    selected_entries = jnp.take(extended, sources, axis=0)
    return (
        jnp.einsum("dfox,dfxk->dok", blocks, selected_entries, precision=highest_accuracy)
        * keep_mask
    )


def adjoint_apply(pixel_field, blocks, sources, keep_mask):
    share_amount = jnp.einsum(
        "yerj,yri->yeji", blocks, pixel_field * keep_mask, precision=highest_accuracy
    )
    positions = jnp.arange(TILES + 4)
    selector = (sources[:, :, None] == positions[None, None, :]).astype(jnp.float32)
    spread = jnp.einsum("tse,tsbc->ebc", selector, share_amount, precision=highest_accuracy)
    lon_padded = lon_edges(spread[TILES : TILES + 2])
    lat_padded = lat_edges(spread[TILES + 2 : TILES + 4])
    edges = jnp.concatenate(
        [lon_padded[0:1], lon_padded[3:4], lat_padded[0:1], lat_padded[3:4]], axis=0
    )
    local = spread[:TILES]
    return jnp.concatenate([local[:4] + edges, local[4:]], axis=0) * keep_mask


def recurrence(start, blocks, sources, keep_mask):
    terms = [start, forward_apply(start, blocks, sources, keep_mask)]
    for order in range(2, CHEB):
        terms.append(2.0 * forward_apply(terms[-1], blocks, sources, keep_mask) - terms[-2])
    return terms


def mix_split(term, weight_row, goal, scale):
    piece = lax.all_gather(term, "ch", axis=2, tiled=True)
    total = jnp.einsum("tpc,co->tpo", piece, weight_row, precision=highest_accuracy)
    part_grad = jnp.einsum("tpc,tpo->co", piece, goal, precision=highest_accuracy) * scale
    return (total, part_grad)


def shards(features, blocks, sources, live, weights, cotangent):
    local_in = features.shape[1]
    local_out = weights.shape[2]
    keep_mask = (jnp.arange(TILES) < live[0]).astype(jnp.float32)[:, None, None]
    pixel_field = features.reshape(TILES, TILE, local_in) * keep_mask
    goal = cotangent.reshape(TILES, TILE, local_out) * keep_mask
    scale = float(TILES * TILE * lax.axis_size("lon") * lax.axis_size("lat")) ** (-0.5)
    terms = recurrence(pixel_field, blocks, sources, keep_mask)
    output = jnp.zeros((TILES, TILE, local_out), jnp.float32)
    grads = []
    for order in range(CHEB):
        mixed, grad = mix_split(terms[order], weights[order], goal, scale)
        output = output + mixed
        grads.append(grad)
    weight_grad = jnp.stack(grads)
    weight_grad = lax.psum(weight_grad, ("lon", "lat"))
    partial_adjoint = jnp.einsum("tpo,kco->ktpc", goal, weights, precision=highest_accuracy)
    summed = lax.psum_scatter(partial_adjoint, "ch", scatter_dimension=3, tiled=True)
    adjoint = [summed[order] for order in range(CHEB)]
    for order in range(CHEB - 1, 1, -1):
        adjoint[order - 1] = adjoint[order - 1] + 2.0 * adjoint_apply(
            adjoint[order], blocks, sources, keep_mask
        )
        adjoint[order - 2] = adjoint[order - 2] - adjoint[order]
    adjoint[0] = adjoint[0] + adjoint_apply(adjoint[1], blocks, sources, keep_mask)
    input_grad = (adjoint[0] * keep_mask).reshape(TILES * TILE, local_in)
    return (output.reshape(TILES * TILE, local_out), input_grad, weight_grad)


def solution(mesh):
    placed = (
        P(("groups", "lon", "lat"), "ch"),
        P(("lon", "lat"), None, None, None),
        P(("lon", "lat"), None),
        P(("lon", "lat")),
        P(None, None, "ch"),
        P(("groups", "lon", "lat"), "ch"),
    )
    return jax.shard_map(
        shards,
        mesh=mesh,
        in_specs=placed,
        out_specs=(
            P(("groups", "lon", "lat"), "ch"),
            P(("groups", "lon", "lat"), "ch"),
            P("groups", None, "ch"),
        ),
        check_vma=False,
    )
```

profile of v0, /device:TPU:0, one launch (start us, length us, event | category | flops | bytes accessed | tf_op | source)
XLA Modules:
  0.0 199.8 jit_solution(17478462229392317581)
XLA Ops:
  8.8 1.2 copy.57
  10.0 5.4 %convolution_bitcast_fusion = f32[4,6,128,256]{2,3,1,0:T(8,128)} fusion(f32[4,256,128]{2,1,0:T(8,128)} %param.12, f32[6,128,128]{1,2,0:T(8,128)S(1)} %copy.57, f32[6]{0:T(128)S(1)} %compare_convert_fusion), kind=kOutput, calls=%fused_computation.3 | convolution fusion | flops 1208057856 | bytes 4063256 | tf_op jit(solution)/shard_map/tpo,kco->ktpc/dot_general | solution.py:94
  16.5 1.3 collective-permute-start.3
  17.8 4.8 %collective-permute-start.2 = (f32[1,128,128]{2,1,0:T(8,128)S(1)}, f32[1,128,128]{2,1,0:T(8,128)S(1)}, u32[]{:S(2)}, u32[]{:S(2)}) collective-permute-start(f32[1,128,128]{2,1,0:T(8,128)S(1)} %get-tuple-element.29), channel_id=1, source_target_pairs={{0,2},{1,3},{4,6},{5,7},{8,10},{9,11},{12,14},{13,15},{16,18},{17,... | collective-permute-start | bytes 196616 | tf_op jit(solution)/shard_map/ppermute | solution.py:21
  22.7 4.8 %collective-permute-start.1 = (f32[1,128,128]{2,1,0:T(8,128)S(1)}, f32[1,128,128]{2,1,0:T(8,128)S(1)}, u32[]{:S(2)}, u32[]{:S(2)}) collective-permute-start(f32[1,128,128]{2,1,0:T(8,128)S(1)} %get-tuple-element.30), channel_id=1, source_target_pairs={{4,0},{8,4},{12,8},{0,12},{5,1},{9,5},{13,9},{1,13},{6,2},{10,6},{... | collective-permute-start | bytes 196616 | tf_op jit(solution)/shard_map/ppermute | solution.py:22
  28.3 2.4 %all_gather.12 = f32[6,128,256]{2,1,0:T(8,128)S(1)} all-gather(f32[6,128,128]{2,1,0:T(8,128)S(1)} %get-tuple-element.5), channel_id=1, replica_groups=mesh['groups'=2,'lon'=4,'lat'=2,'ch'=2] {'ch'}, dimensions={2}, use_global_device_ids=true | all-gather | bytes 1179648 | tf_op jit(solution)/shard_map/all_gather | solution.py:72
  30.7 2.1 %fusion.35 = f32[1,256,128]{2,1,0:T(8,128)} fusion(f32[6,128,256]{2,1,0:T(8,128)S(1)} %all_gather.12, f32[6,128,128]{1,2,0:T(8,128)S(1)} %copy.57, f32[6]{0:T(128)S(1)} %compare_convert_fusion), kind=kOutput, calls=%fused_computation.43 | convolution fusion | flops 302120960 | bytes 1310744 | tf_op jit(solution)/shard_map/tpc,tpo->co/dot_general | solution.py:74
  32.9 2.4 %fusion.86 = f32[6,128,128]{2,1,0:T(8,128)} fusion(f32[6,128,256]{2,1,0:T(8,128)S(1)} %all_gather.12, f32[4,256,128]{2,1,0:T(8,128)} %param.12), kind=kOutput, calls=%fused_computation.104 | convolution fusion | flops 301989888 | bytes 1310720 | tf_op jit(solution)/shard_map/tpc,co->tpo/dot_general | solution.py:73
  35.4 1.7 gather_fusion
  37.1 1.6 copy.47
  38.7 3.2 %constant_dynamic-update-slice_fusion.9 = (f32[10,128,128]{2,1,0:T(8,128)}, f32[6,128,128]{2,1,0:T(8,128)S(1)}) fusion(f32[6]{0:T(128)S(1)} %compare_convert_fusion, f32[6,3,128,128]{3,2,1,0:T(8,128)S(1)} %copy-done, f32[6,3,128,128]{2,3,1,0:T(8,128)S(1)} %copy.47, pred[6,3]{1,0:T(8,128)(4,1)} %copy.45), kind=kOutput, calls=%fused_computation.119 | convolution fusion | flops 453378048 | bytes 3145770 | tf_op jit(solution)/shard_map/dfox,dfxk->dok/dot_general | solution.py:43
  42.0 2.5 %all_gather.13 = f32[6,128,256]{2,1,0:T(8,128)S(1)} all-gather(f32[6,128,128]{2,1,0:T(8,128)S(1)} %get-tuple-element.33), channel_id=1, replica_groups=mesh['groups'=2,'lon'=4,'lat'=2,'ch'=2] {'ch'}, dimensions={2}, use_global_device_ids=true | all-gather | bytes 1179648 | tf_op jit(solution)/shard_map/all_gather | solution.py:72
  44.5 2.4 %convolution_add_fusion.2 = f32[6,128,128]{2,1,0:T(8,128)} fusion(f32[6,128,128]{2,1,0:T(8,128)S(1)} %copy-done.5, f32[6,128,256]{2,1,0:T(8,128)S(1)} %all_gather.13, f32[4,256,128]{2,1,0:T(8,128)} %param.12), kind=kOutput, calls=%fused_computation.18 | convolution fusion | flops 302088192 | bytes 1703936 | tf_op jit(solution)/shard_map/tpc,co->tpo/dot_general | solution.py:73
  46.9 2.1 %fusion.33 = f32[1,256,128]{2,1,0:T(8,128)} fusion(f32[6,128,256]{2,1,0:T(8,128)S(1)} %all_gather.13, f32[6,128,128]{1,2,0:T(8,128)S(1)} %copy.57, f32[6]{0:T(128)S(1)} %compare_convert_fusion), kind=kOutput, calls=%fused_computation.40 | convolution fusion | flops 302120960 | bytes 1310744 | tf_op jit(solution)/shard_map/tpc,tpo->co/dot_general | solution.py:74
  49.0 1.3 collective-permute-start.7
  50.3 4.5 %collective-permute-start.6 = (f32[1,128,128]{2,1,0:T(8,128)S(1)}, f32[1,128,128]{2,1,0:T(8,128)S(1)}, u32[]{:S(2)}, u32[]{:S(2)}) collective-permute-start(f32[1,128,128]{2,1,0:T(8,128)S(1)} %get-tuple-element.25), channel_id=1, source_target_pairs={{0,2},{1,3},{4,6},{5,7},{8,10},{9,11},{12,14},{13,15},{16,18},{17,... | collective-permute-start | bytes 196616 | tf_op jit(solution)/shard_map/ppermute | solution.py:21
  54.9 4.1 %collective-permute-start.5 = (f32[1,128,128]{2,1,0:T(8,128)S(1)}, f32[1,128,128]{2,1,0:T(8,128)S(1)}, u32[]{:S(2)}, u32[]{:S(2)}) collective-permute-start(f32[1,128,128]{2,1,0:T(8,128)S(1)} %get-tuple-element.26), channel_id=1, source_target_pairs={{4,0},{8,4},{12,8},{0,12},{5,1},{9,5},{13,9},{1,13},{6,2},{10,6},{... | collective-permute-start | bytes 196616 | tf_op jit(solution)/shard_map/ppermute | solution.py:22
  59.6 1.3 collective-permute-done.5
  62.8 1.7 gather_fusion.1
  64.5 1.4 copy.51
  65.9 2.9 %constant_dynamic-update-slice_fusion.14 = (f32[10,128,128]{2,1,0:T(8,128)S(1)}, f32[6,128,128]{2,1,0:T(8,128)S(1)}) fusion(f32[6,128,128]{2,1,0:T(8,128)S(1)} %get-tuple-element.5, f32[6]{0:T(128)S(1)} %compare_convert_fusion, f32[6,3,128,128]{3,2,1,0:T(8,128)S(1)} %copy-done, f32[6,3,128,128]{2,3,1,0:T(8,128)} %copy.51, pred[6,3]{1,0:T(8,128)(4,1)} %copy.45), kind=kOutput, calls=%fused_computation.124 | convolution fusion | flops 453574656 | bytes 3538986 | tf_op jit(solution)/shard_map/dfox,dfxk->dok/dot_general | solution.py:43
  68.9 1.4 collective-permute-start.8
  70.3 2.4 %all_gather.14 = f32[6,128,256]{2,1,0:T(8,128)S(1)} all-gather(f32[6,128,128]{2,1,0:T(8,128)S(1)} %get-tuple-element.35), channel_id=1, replica_groups=mesh['groups'=2,'lon'=4,'lat'=2,'ch'=2] {'ch'}, dimensions={2}, use_global_device_ids=true | all-gather | bytes 1179648 | tf_op jit(solution)/shard_map/all_gather | solution.py:72
  72.6 2.4 %convolution_add_fusion.1 = f32[6,128,128]{2,1,0:T(8,128)} fusion(f32[6,128,128]{2,1,0:T(8,128)S(1)} %copy-done.6, f32[6,128,256]{2,1,0:T(8,128)S(1)} %all_gather.14, f32[4,256,128]{2,1,0:T(8,128)} %param.12), kind=kOutput, calls=%fused_computation.17 | convolution fusion | flops 302088192 | bytes 1703936 | tf_op jit(solution)/shard_map/tpc,co->tpo/dot_general | solution.py:73
  75.0 2.1 %fusion.31 = f32[1,256,128]{2,1,0:T(8,128)} fusion(f32[6,128,256]{2,1,0:T(8,128)S(1)} %all_gather.14, f32[6,128,128]{1,2,0:T(8,128)S(1)} %copy.57, f32[6]{0:T(128)S(1)} %compare_convert_fusion), kind=kOutput, calls=%fused_computation.37 | convolution fusion | flops 302120960 | bytes 1310744 | tf_op jit(solution)/shard_map/tpc,tpo->co/dot_general | solution.py:74
  77.1 1.3 collective-permute-start.11
  78.4 4.5 %collective-permute-start.10 = (f32[1,128,128]{2,1,0:T(8,128)S(1)}, f32[1,128,128]{2,1,0:T(8,128)S(1)}, u32[]{:S(2)}, u32[]{:S(2)}) collective-permute-start(f32[1,128,128]{2,1,0:T(8,128)S(1)} %get-tuple-element.21), channel_id=1, source_target_pairs={{0,2},{1,3},{4,6},{5,7},{8,10},{9,11},{12,14},{13,15},{16,18},{17,... | collective-permute-start | bytes 196616 | tf_op jit(solution)/shard_map/ppermute | solution.py:21
  83.0 3.1 %collective-permute-start.9 = (f32[1,128,128]{2,1,0:T(8,128)S(1)}, f32[1,128,128]{2,1,0:T(8,128)S(1)}, u32[]{:S(2)}, u32[]{:S(2)}) collective-permute-start(f32[1,128,128]{2,1,0:T(8,128)S(1)} %get-tuple-element.22), channel_id=1, source_target_pairs={{4,0},{8,4},{12,8},{0,12},{5,1},{9,5},{13,9},{1,13},{6,2},{10,6},{... | collective-permute-start | bytes 196616 | tf_op jit(solution)/shard_map/ppermute | solution.py:22
  86.1 1.9 collective-permute-done.9
  88.0 1.7 gather_fusion.2
  89.7 1.6 copy.55
  91.3 1.7 fusion.24
  93.1 2.7 %all_gather.15 = f32[6,128,256]{2,1,0:T(8,128)S(1)} all-gather(f32[6,128,128]{2,1,0:T(8,128)S(1)} %fusion.24), channel_id=1, replica_groups=mesh['groups'=2,'lon'=4,'lat'=2,'ch'=2] {'ch'}, dimensions={2}, use_global_device_ids=true | all-gather | bytes 1179648 | tf_op jit(solution)/shard_map/all_gather | solution.py:72
  95.8 1.4 fusion.29
  97.2 2.4 %convolution_add_fusion = f32[6,128,128]{2,1,0:T(8,128)} fusion(f32[6,128,128]{2,1,0:T(8,128)S(1)} %copy-done.7, f32[6,128,256]{2,1,0:T(8,128)S(1)} %all_gather.15, f32[4,256,128]{2,1,0:T(8,128)} %param.12), kind=kOutput, calls=%fused_computation.16 | convolution fusion | flops 302088192 | bytes 1703936 | tf_op jit(solution)/shard_map/tpc,co->tpo/dot_general | solution.py:73
  99.7 3.2 %fusion.55 = f32[6,128,3,128]{3,1,2,0:T(8,128)} fusion(f32[6,3,128,128]{3,2,1,0:T(8,128)S(1)} %copy-done, f32[4,6,128,128]{2,3,1,0:T(8,128)} %reduce-scatter.2.cloned.1.call-done, f32[6]{0:T(128)S(1)} %compare_convert_fusion), kind=kOutput, calls=%fused_computation.67 | convolution fusion | flops 453083136 | bytes 2752536 | tf_op jit(solution)/shard_map/yerj,yri->yeji/dot_general | solution.py:49
  102.9 1.8 copy.91
  104.7 1.1 fusion.6
  107.4 4.2 %collective-permute-start.13 = (f32[1,128,128]{1,2,0:T(8,128)S(1)}, f32[1,128,128]{1,2,0:T(8,128)S(1)}, u32[]{:S(2)}, u32[]{:S(2)}) collective-permute-start(f32[1,128,128]{1,2,0:T(8,128)S(1)} %copy.113), channel_id=1, source_target_pairs={{4,0},{8,4},{12,8},{0,12},{5,1},{9,5},{13,9},{1,13},{6,2},{10,6},{... | collective-permute-start | bytes 196616 | tf_op jit(solution)/shard_map/ppermute | solution.py:22
  111.6 1.3 collective-permute-start.14
  112.9 1.3 collective-permute-start.15
  115.2 1.1 slice.223
  116.3 1.1 slice.218
  117.6 1.5 collective-permute-done.15
  119.1 1.3 collective-permute-done.12
  120.4 3.2 %fusion.53 = f32[6,128,3,128]{3,1,2,0:T(8,128)} fusion(f32[6,3,128,128]{3,2,1,0:T(8,128)S(1)} %copy-done, f32[6]{0:T(128)S(1)} %compare_convert_fusion, f32[4,6,128,128]{2,3,1,0:T(8,128)} %reduce-scatter.2.cloned.1.call-done, f32[2,128,128]{1,2,0:T(8,128)S(1)} %copy.116, f32[4,128,128]{1,2,0:T(8,128)S(1)} %maximum_add_fusion), kind=kOutput, calls=%fused_computation.65 | convolution fusion | flops 453476352 | bytes 3145752 | tf_op jit(solution)/shard_map/yerj,yri->yeji/dot_general | solution.py:49
  123.6 1.8 copy.94
  125.4 1.1 fusion.9
  128.1 1.2 collective-permute-start.17
  129.3 4.6 %collective-permute-start.18 = (f32[1,128,128]{1,2,0:T(8,128)S(1)}, f32[1,128,128]{1,2,0:T(8,128)S(1)}, u32[]{:S(2)}, u32[]{:S(2)}) collective-permute-start(f32[1,128,128]{1,2,0:T(8,128)S(1)} %copy.120), channel_id=1, source_target_pairs={{0,2},{1,3},{4,6},{5,7},{8,10},{9,11},{12,14},{13,15},{16,18},{17,... | collective-permute-start | bytes 196616 | tf_op jit(solution)/shard_map/ppermute | solution.py:21
  133.9 1.3 collective-permute-start.19
  135.2 1.2 collective-permute-start.16
  136.3 1.2 fusion.106
  138.6 1.1 slice.230
  141.6 3.4 %fusion.47 = f32[6,128,3,128]{3,1,2,0:T(8,128)} fusion(f32[6,3,128,128]{3,2,1,0:T(8,128)S(1)} %copy-done, f32[4,6,128,128]{2,3,1,0:T(8,128)} %reduce-scatter.2.cloned.1.call-done, f32[2,128,128]{1,2,0:T(8,128)S(1)} %copy.122, f32[4,128,128]{1,2,0:T(8,128)S(1)} %maximum_add_fusion.1, f32[6]{0:T(128)S(1)} %compare_convert_fusion), kind=kOutput, calls=%fused_computation.58 | convolution fusion | flops 453574656 | bytes 3538968 | tf_op jit(solution)/shard_map/yerj,yri->yeji/dot_general | solution.py:49
  144.9 1.8 copy.97
  146.7 1.1 fusion.12
  149.1 1.3 collective-permute-start.23
  150.4 4.6 %collective-permute-start.22 = (f32[1,128,128]{2,0,1:T(1,128)S(1)}, f32[1,128,128]{2,0,1:T(1,128)S(1)}, u32[]{:S(2)}, u32[]{:S(2)}) collective-permute-start(f32[1,128,128]{2,0,1:T(1,128)S(1)} %get-tuple-element.10), channel_id=1, source_target_pairs={{0,2},{1,3},{4,6},{5,7},{8,10},{9,11},{12,14},{13,15},{16,18},{17,... | collective-permute-start | bytes 196616 | tf_op jit(solution)/shard_map/ppermute | solution.py:21
  155.0 3.9 %collective-permute-start.21 = (f32[1,128,128]{2,0,1:T(1,128)S(1)}, f32[1,128,128]{2,0,1:T(1,128)S(1)}, u32[]{:S(2)}, u32[]{:S(2)}) collective-permute-start(f32[1,128,128]{2,0,1:T(1,128)S(1)} %get-tuple-element.11), channel_id=1, source_target_pairs={{4,0},{8,4},{12,8},{0,12},{5,1},{9,5},{13,9},{1,13},{6,2},{10,6},{... | collective-permute-start | bytes 196616 | tf_op jit(solution)/shard_map/ppermute | solution.py:22
  159.0 1.1 slice.236
  160.8 1.3 slice_add_fusion
  163.2 27.3 %all-reduce.2.cloned.1.call-done = f32[4,256,128]{2,1,0:T(8,128)} async-done(((f32[4,256,128]{2,1,0:T(8,128)}), f32[4,256,128]{2,1,0:T(8,128)}) %all-reduce.2.cloned.1.call-update) | async-done | bytes 524304 | tf_op jit(solution)/shard_map/psum | solution.py:93
  190.5 1.9 copy.137
  (107 shorter events, 15.2 us)
Async XLA Ops:
  8.0 30.7 %copy-start = (f32[6,3,128,128]{3,2,1,0:T(8,128)S(1)}, f32[6,3,128,128]{3,2,1,0:T(8,128)}, u32[]{:S(2)}) copy-start(f32[6,3,128,128]{3,2,1,0:T(8,128)} %param.9) | copy-start | bytes 3538948
  8.0 91.7 %reduce-scatter.2.cloned.1.call-start = ((), (), s32[]{:S(2)}) async-start(), calls=%async_computation.1 | async-start | bytes 4718592 | tf_op jit(solution)/shard_map/reduce_scatter | solution.py:95
  15.4 1.0 copy-start.11
  15.4 12.1 %copy-start.12 = (s32[6,3]{0,1:T(4,128)S(1)}, s32[6,3]{0,1:T(4,128)}, u32[]{:S(2)}) copy-start(s32[6,3]{0,1:T(4,128)} %param.10) | copy-start | bytes 220
  15.4 175.1 %all-reduce.2.cloned.1.call-start = ((), (), s32[]{:S(2)}) async-start(), calls=%async_computation.2 | async-start | bytes 1048576 | tf_op jit(solution)/shard_map/psum | solution.py:93
  16.5 18.9 %collective-permute-start.3 = (f32[1,128,128]{2,1,0:T(8,128)S(1)}, f32[1,128,128]{2,1,0:T(8,128)S(1)}, u32[]{:S(2)}, u32[]{:S(2)}) collective-permute-start(f32[1,128,128]{2,1,0:T(8,128)S(1)} %get-tuple-element.28), channel_id=1, source_target_pairs={{2,0},{3,1},{6,4},{7,5},{10,8},{11,9},{14,12},{15,13},{18,16},{19,... | collective-permute-start | bytes 196616 | tf_op jit(solution)/shard_map/ppermute | solution.py:22
  17.8 17.5 %collective-permute-start.2 = (f32[1,128,128]{2,1,0:T(8,128)S(1)}, f32[1,128,128]{2,1,0:T(8,128)S(1)}, u32[]{:S(2)}, u32[]{:S(2)}) collective-permute-start(f32[1,128,128]{2,1,0:T(8,128)S(1)} %get-tuple-element.29), channel_id=1, source_target_pairs={{0,2},{1,3},{4,6},{5,7},{8,10},{9,11},{12,14},{13,15},{16,18},{17,... | collective-permute-start | bytes 196616 | tf_op jit(solution)/shard_map/ppermute | solution.py:21
  22.7 12.7 %collective-permute-start.1 = (f32[1,128,128]{2,1,0:T(8,128)S(1)}, f32[1,128,128]{2,1,0:T(8,128)S(1)}, u32[]{:S(2)}, u32[]{:S(2)}) collective-permute-start(f32[1,128,128]{2,1,0:T(8,128)S(1)} %get-tuple-element.30), channel_id=1, source_target_pairs={{4,0},{8,4},{12,8},{0,12},{5,1},{9,5},{13,9},{1,13},{6,2},{10,6},{... | collective-permute-start | bytes 196616 | tf_op jit(solution)/shard_map/ppermute | solution.py:22
  27.5 7.8 %collective-permute-start = (f32[1,128,128]{2,1,0:T(8,128)S(1)}, f32[1,128,128]{2,1,0:T(8,128)S(1)}, u32[]{:S(2)}, u32[]{:S(2)}) collective-permute-start(f32[1,128,128]{2,1,0:T(8,128)S(1)} %get-tuple-element.31), channel_id=1, source_target_pairs={{0,4},{4,8},{8,12},{12,0},{1,5},{5,9},{9,13},{13,1},{2,6},{6,10},{... | collective-permute-start | bytes 196616 | tf_op jit(solution)/shard_map/ppermute | solution.py:21
  41.9 2.6 %copy-start.5 = (f32[6,128,128]{2,1,0:T(8,128)S(1)}, f32[6,128,128]{2,1,0:T(8,128)}, u32[]{:S(2)}) copy-start(f32[6,128,128]{2,1,0:T(8,128)} %fusion.86) | copy-start | bytes 1179652
  41.9 17.0 %collective-permute-start.4 = (f32[1,128,128]{2,1,0:T(8,128)S(1)}, f32[1,128,128]{2,1,0:T(8,128)S(1)}, u32[]{:S(2)}, u32[]{:S(2)}) collective-permute-start(f32[1,128,128]{2,1,0:T(8,128)S(1)} %get-tuple-element.27), channel_id=1, source_target_pairs={{0,4},{4,8},{8,12},{12,0},{1,5},{5,9},{9,13},{13,1},{2,6},{6,10},{... | collective-permute-start | bytes 196616 | tf_op jit(solution)/shard_map/ppermute | solution.py:21
  49.0 13.1 %collective-permute-start.7 = (f32[1,128,128]{2,1,0:T(8,128)S(1)}, f32[1,128,128]{2,1,0:T(8,128)S(1)}, u32[]{:S(2)}, u32[]{:S(2)}) collective-permute-start(f32[1,128,128]{2,1,0:T(8,128)S(1)} %get-tuple-element.24), channel_id=1, source_target_pairs={{2,0},{3,1},{6,4},{7,5},{10,8},{11,9},{14,12},{15,13},{18,16},{19,... | collective-permute-start | bytes 196616 | tf_op jit(solution)/shard_map/ppermute | solution.py:22
  50.3 11.2 %collective-permute-start.6 = (f32[1,128,128]{2,1,0:T(8,128)S(1)}, f32[1,128,128]{2,1,0:T(8,128)S(1)}, u32[]{:S(2)}, u32[]{:S(2)}) collective-permute-start(f32[1,128,128]{2,1,0:T(8,128)S(1)} %get-tuple-element.25), channel_id=1, source_target_pairs={{0,2},{1,3},{4,6},{5,7},{8,10},{9,11},{12,14},{13,15},{16,18},{17,... | collective-permute-start | bytes 196616 | tf_op jit(solution)/shard_map/ppermute | solution.py:21
  54.9 6.0 %collective-permute-start.5 = (f32[1,128,128]{2,1,0:T(8,128)S(1)}, f32[1,128,128]{2,1,0:T(8,128)S(1)}, u32[]{:S(2)}, u32[]{:S(2)}) collective-permute-start(f32[1,128,128]{2,1,0:T(8,128)S(1)} %get-tuple-element.26), channel_id=1, source_target_pairs={{4,0},{8,4},{12,8},{0,12},{5,1},{9,5},{13,9},{1,13},{6,2},{10,6},{... | collective-permute-start | bytes 196616 | tf_op jit(solution)/shard_map/ppermute | solution.py:22
  68.8 3.8 %copy-start.6 = (f32[6,128,128]{2,1,0:T(8,128)S(1)}, f32[6,128,128]{2,1,0:T(8,128)}, u32[]{:S(2)}) copy-start(f32[6,128,128]{2,1,0:T(8,128)} %convolution_add_fusion.2) | copy-start | bytes 1179652
  68.9 17.2 %collective-permute-start.8 = (f32[1,128,128]{2,1,0:T(8,128)S(1)}, f32[1,128,128]{2,1,0:T(8,128)S(1)}, u32[]{:S(2)}, u32[]{:S(2)}) collective-permute-start(f32[1,128,128]{2,1,0:T(8,128)S(1)} %get-tuple-element.23), channel_id=1, source_target_pairs={{0,4},{4,8},{8,12},{12,0},{1,5},{5,9},{9,13},{13,1},{2,6},{6,10},{... | collective-permute-start | bytes 196616 | tf_op jit(solution)/shard_map/ppermute | solution.py:21
  77.1 10.8 %collective-permute-start.11 = (f32[1,128,128]{2,1,0:T(8,128)S(1)}, f32[1,128,128]{2,1,0:T(8,128)S(1)}, u32[]{:S(2)}, u32[]{:S(2)}) collective-permute-start(f32[1,128,128]{2,1,0:T(8,128)S(1)} %get-tuple-element.20), channel_id=1, source_target_pairs={{2,0},{3,1},{6,4},{7,5},{10,8},{11,9},{14,12},{15,13},{18,16},{19,... | collective-permute-start | bytes 196616 | tf_op jit(solution)/shard_map/ppermute | solution.py:22
  78.4 9.5 %collective-permute-start.10 = (f32[1,128,128]{2,1,0:T(8,128)S(1)}, f32[1,128,128]{2,1,0:T(8,128)S(1)}, u32[]{:S(2)}, u32[]{:S(2)}) collective-permute-start(f32[1,128,128]{2,1,0:T(8,128)S(1)} %get-tuple-element.21), channel_id=1, source_target_pairs={{0,2},{1,3},{4,6},{5,7},{8,10},{9,11},{12,14},{13,15},{16,18},{17,... | collective-permute-start | bytes 196616 | tf_op jit(solution)/shard_map/ppermute | solution.py:21
  83.0 5.0 %collective-permute-start.9 = (f32[1,128,128]{2,1,0:T(8,128)S(1)}, f32[1,128,128]{2,1,0:T(8,128)S(1)}, u32[]{:S(2)}, u32[]{:S(2)}) collective-permute-start(f32[1,128,128]{2,1,0:T(8,128)S(1)} %get-tuple-element.22), channel_id=1, source_target_pairs={{4,0},{8,4},{12,8},{0,12},{5,1},{9,5},{13,9},{1,13},{6,2},{10,6},{... | collective-permute-start | bytes 196616 | tf_op jit(solution)/shard_map/ppermute | solution.py:22
  89.7 1.7 copy-start.13
  93.0 4.2 %copy-start.7 = (f32[6,128,128]{2,1,0:T(8,128)S(1)}, f32[6,128,128]{2,1,0:T(8,128)}, u32[]{:S(2)}) copy-start(f32[6,128,128]{2,1,0:T(8,128)} %convolution_add_fusion.1) | copy-start | bytes 1179652
  104.7 9.6 %copy-start.8 = (f32[1,256,128]{2,1,0:T(8,128)S(1)}, f32[1,256,128]{2,1,0:T(8,128)}, u32[]{:S(2)}) copy-start(f32[1,256,128]{2,1,0:T(8,128)} %fusion.35) | copy-start | bytes 393220
  104.7 9.6 %copy-start.9 = (f32[1,256,128]{2,1,0:T(8,128)S(1)}, f32[1,256,128]{2,1,0:T(8,128)}, u32[]{:S(2)}) copy-start(f32[1,256,128]{2,1,0:T(8,128)} %fusion.33) | copy-start | bytes 393220
  104.7 9.6 %copy-start.10 = (f32[1,256,128]{2,1,0:T(8,128)S(1)}, f32[1,256,128]{2,1,0:T(8,128)}, u32[]{:S(2)}) copy-start(f32[1,256,128]{2,1,0:T(8,128)} %fusion.31) | copy-start | bytes 393220
  105.8 1.0 copy-start.1
  107.4 10.2 %collective-permute-start.13 = (f32[1,128,128]{1,2,0:T(8,128)S(1)}, f32[1,128,128]{1,2,0:T(8,128)S(1)}, u32[]{:S(2)}, u32[]{:S(2)}) collective-permute-start(f32[1,128,128]{1,2,0:T(8,128)S(1)} %copy.113), channel_id=1, source_target_pairs={{4,0},{8,4},{12,8},{0,12},{5,1},{9,5},{13,9},{1,13},{6,2},{10,6},{... | collective-permute-start | bytes 196616 | tf_op jit(solution)/shard_map/ppermute | solution.py:22
  111.6 6.0 %collective-permute-start.14 = (f32[1,128,128]{1,2,0:T(8,128)S(1)}, f32[1,128,128]{1,2,0:T(8,128)S(1)}, u32[]{:S(2)}, u32[]{:S(2)}) collective-permute-start(f32[1,128,128]{1,2,0:T(8,128)S(1)} %copy.114), channel_id=1, source_target_pairs={{0,2},{1,3},{4,6},{5,7},{8,10},{9,11},{12,14},{13,15},{16,18},{17,... | collective-permute-start | bytes 196616 | tf_op jit(solution)/shard_map/ppermute | solution.py:21
  112.9 6.2 %collective-permute-start.15 = (f32[1,128,128]{1,2,0:T(8,128)S(1)}, f32[1,128,128]{1,2,0:T(8,128)S(1)}, u32[]{:S(2)}, u32[]{:S(2)}) collective-permute-start(f32[1,128,128]{1,2,0:T(8,128)S(1)} %copy.115), channel_id=1, source_target_pairs={{2,0},{3,1},{6,4},{7,5},{10,8},{11,9},{14,12},{15,13},{18,16},{19,... | collective-permute-start | bytes 196616 | tf_op jit(solution)/shard_map/ppermute | solution.py:22
  114.2 6.1 %collective-permute-start.12 = (f32[1,128,128]{1,2,0:T(8,128)S(1)}, f32[1,128,128]{1,2,0:T(8,128)S(1)}, u32[]{:S(2)}, u32[]{:S(2)}) collective-permute-start(f32[1,128,128]{1,2,0:T(8,128)S(1)} %copy.112), channel_id=1, source_target_pairs={{0,4},{4,8},{8,12},{12,0},{1,5},{5,9},{9,13},{13,1},{2,6},{6,10},{... | collective-permute-start | bytes 196616 | tf_op jit(solution)/shard_map/ppermute | solution.py:21
  126.5 1.0 copy-start.3
  128.1 12.9 %collective-permute-start.17 = (f32[1,128,128]{1,2,0:T(8,128)S(1)}, f32[1,128,128]{1,2,0:T(8,128)S(1)}, u32[]{:S(2)}, u32[]{:S(2)}) collective-permute-start(f32[1,128,128]{1,2,0:T(8,128)S(1)} %copy.119), channel_id=1, source_target_pairs={{4,0},{8,4},{12,8},{0,12},{5,1},{9,5},{13,9},{1,13},{6,2},{10,6},{... | collective-permute-start | bytes 196616 | tf_op jit(solution)/shard_map/ppermute | solution.py:22
  129.3 11.8 %collective-permute-start.18 = (f32[1,128,128]{1,2,0:T(8,128)S(1)}, f32[1,128,128]{1,2,0:T(8,128)S(1)}, u32[]{:S(2)}, u32[]{:S(2)}) collective-permute-start(f32[1,128,128]{1,2,0:T(8,128)S(1)} %copy.120), channel_id=1, source_target_pairs={{0,2},{1,3},{4,6},{5,7},{8,10},{9,11},{12,14},{13,15},{16,18},{17,... | collective-permute-start | bytes 196616 | tf_op jit(solution)/shard_map/ppermute | solution.py:21
  133.9 7.2 %collective-permute-start.19 = (f32[1,128,128]{1,2,0:T(8,128)S(1)}, f32[1,128,128]{1,2,0:T(8,128)S(1)}, u32[]{:S(2)}, u32[]{:S(2)}) collective-permute-start(f32[1,128,128]{1,2,0:T(8,128)S(1)} %copy.121), channel_id=1, source_target_pairs={{2,0},{3,1},{6,4},{7,5},{10,8},{11,9},{14,12},{15,13},{18,16},{19,... | collective-permute-start | bytes 196616 | tf_op jit(solution)/shard_map/ppermute | solution.py:22
  135.2 6.4 %collective-permute-start.16 = (f32[1,128,128]{1,2,0:T(8,128)S(1)}, f32[1,128,128]{1,2,0:T(8,128)S(1)}, u32[]{:S(2)}, u32[]{:S(2)}) collective-permute-start(f32[1,128,128]{1,2,0:T(8,128)S(1)} %copy.118), channel_id=1, source_target_pairs={{0,4},{4,8},{8,12},{12,0},{1,5},{5,9},{9,13},{13,1},{2,6},{6,10},{... | collective-permute-start | bytes 196616 | tf_op jit(solution)/shard_map/ppermute | solution.py:21
  147.8 1.0 copy-start.2
  149.0 11.1 %collective-permute-start.20 = (f32[1,128,128]{2,0,1:T(1,128)S(1)}, f32[1,128,128]{2,0,1:T(1,128)S(1)}, u32[]{:S(2)}, u32[]{:S(2)}) collective-permute-start(f32[1,128,128]{2,0,1:T(1,128)S(1)} %get-tuple-element.8), channel_id=1, source_target_pairs={{0,4},{4,8},{8,12},{12,0},{1,5},{5,9},{9,13},{13,1},{2,6},{6,10},{... | collective-permute-start | bytes 196616 | tf_op jit(solution)/shard_map/ppermute | solution.py:21
  149.1 11.0 %collective-permute-start.23 = (f32[1,128,128]{2,0,1:T(1,128)S(1)}, f32[1,128,128]{2,0,1:T(1,128)S(1)}, u32[]{:S(2)}, u32[]{:S(2)}) collective-permute-start(f32[1,128,128]{2,0,1:T(1,128)S(1)} %get-tuple-element.9), channel_id=1, source_target_pairs={{2,0},{3,1},{6,4},{7,5},{10,8},{11,9},{14,12},{15,13},{18,16},{19,... | collective-permute-start | bytes 196616 | tf_op jit(solution)/shard_map/ppermute | solution.py:22
  150.4 9.8 %collective-permute-start.22 = (f32[1,128,128]{2,0,1:T(1,128)S(1)}, f32[1,128,128]{2,0,1:T(1,128)S(1)}, u32[]{:S(2)}, u32[]{:S(2)}) collective-permute-start(f32[1,128,128]{2,0,1:T(1,128)S(1)} %get-tuple-element.10), channel_id=1, source_target_pairs={{0,2},{1,3},{4,6},{5,7},{8,10},{9,11},{12,14},{13,15},{16,18},{17,... | collective-permute-start | bytes 196616 | tf_op jit(solution)/shard_map/ppermute | solution.py:21
  155.0 5.8 %collective-permute-start.21 = (f32[1,128,128]{2,0,1:T(1,128)S(1)}, f32[1,128,128]{2,0,1:T(1,128)S(1)}, u32[]{:S(2)}, u32[]{:S(2)}) collective-permute-start(f32[1,128,128]{2,0,1:T(1,128)S(1)} %get-tuple-element.11), channel_id=1, source_target_pairs={{4,0},{8,4},{12,8},{0,12},{5,1},{9,5},{13,9},{1,13},{6,2},{10,6},{... | collective-permute-start | bytes 196616 | tf_op jit(solution)/shard_map/ppermute | solution.py:22
  160.1 2.2 %copy-start.4 = (f32[1,6,128,128]{3,2,1,0:T(8,128)S(1)}, f32[1,6,128,128]{3,2,1,0:T(8,128)}, u32[]{:S(2)}) copy-start(f32[1,6,128,128]{3,2,1,0:T(8,128)} %copy.61) | copy-start | bytes 1179652
Sparse Core Ops, SparseCore 0:
  15.5 13.6 reduce-scatter.1
Sparse Core Ops, SparseCore 1:
  115.3 75.2 all-reduce.1
where the time goes:
time: 201 us; the launch traced here: 200 us
  starting transfers between devices  56 us (28%)
  matrix products  43.8 us (22%)
  local copies, waits for them, and re-layouts  35.4 us (18%)
  waiting for transfers between devices  34.4 us (17%)
  between operations  16.9 us (8%)
  blocking collectives  9.94 us (5%)
  other arithmetic  3.38 us (2%)
    ppermute x12, starting transfers between devices, padded(): after = lax.ppermute(leading, axis, down)  28.9 us
    psum x1, waiting for transfers between devices, shards(): weight_grad = lax.psum(weight_grad, ('lon', 'lat'))  27.3 us
    ppermute x12, starting transfers between devices, padded(): before = lax.ppermute(last, axis, up)  27.1 us
    all_gather x4, blocking collectives, mix_split(): piece = lax.all_gather(term, 'ch', axis=2, tiled=True)  9.94 us
    dot_general x3, matrix products, adjoint_apply(): jnp.einsum('yerj,yri->yeji', blocks, pixel_field * keep_mask, precision=h...  9.78 us
    dot_general x4, matrix products, mix_split(): jnp.einsum('tpc,co->tpo', piece, weight_row, precision=highest_accuracy)  9.75 us
    gather x6, local copies, waits for them, and re-layouts, forward_apply(): selected_entries = jnp.take(extended, sources, axis=0)  9.73 us
    unnamed x50, local copies, waits for them, and re-layouts  8.95 us
  transfers between devices with their start and end apart: 26, of which 7 were waited for; matrix products, arithmetic and copies ran while one was open for 32% of the time, Pallas kernels for 0%

commit v1 on v0

v1 whole, which is shorter than its diff:
```python
import functools

import jax
import jax.numpy as jnp
from jax import lax
from jax.experimental import pallas as pl
from jax.experimental.pallas import tpu as pltpu
from jax.sharding import PartitionSpec as P

CHEB = 4
TILE = 128
TILES = 6
ROWS = TILE * TILES
MESH = pl.DeviceIdType.MESH
F32 = jnp.float32
BF16 = jnp.bfloat16


def dot(a, b):
    return jnp.dot(a, b, preferred_element_type=F32)


def split(x):
    hi = x.astype(BF16)
    return hi, (x - hi.astype(F32)).astype(BF16)


def kernel(
    n_lon, n_lat, own_lon, scale,
    feat, blocks, src, live, w, cot,
    out, ig, wg,
    fx, f_hi, f_lo, ft_hi, ft_lo, w_hl, wt_hh, wt_lo, bb, bt,
    u, b, s, s_hl, ext, loc, free, sp,
    recv_f, recv_s, ig_acc, ig_send, ig_recv,
    wg_part, rx, wg_x, rz, wg_sum,
    fx_sem, hf_send, hf_recv, hs_send, hs_recv, ig_ssem, ig_rsem,
    rx_send, rx_recv, rz_send, rz_recv, az_send, az_recv, ax_send, ax_recv,
):
    part = 256 // n_lat
    piece = part // own_lon
    ch = lax.axis_index("ch")
    lon = lax.axis_index("lon")
    lat = lax.axis_index("lat")
    west = lax.rem(lon + n_lon - 1, n_lon)
    east = lax.rem(lon + 1, n_lon)
    mine = pl.ds(pl.multiple_of(ch * 128, 128), 128)
    other = pl.ds(pl.multiple_of((1 - ch) * 128, 128), 128)

    def rows(t):
        return pl.ds(t * TILE, TILE)

    def mask(t):
        return (t < live[0]).astype(F32)

    def remote(a, d, ssem, rsem, dev):
        return pltpu.make_async_remote_copy(
            src_ref=a, dst_ref=d, send_sem=ssem, recv_sem=rsem, device_id=dev, device_id_type=MESH
        )

    barrier = pltpu.get_barrier_semaphore()
    pl.semaphore_signal(barrier, inc=1, device_id={"ch": 1 - ch}, device_id_type=MESH)
    for d in range(1, n_lat):
        pl.semaphore_signal(barrier, inc=1, device_id={"lat": lax.rem(lat + d, n_lat)}, device_id_type=MESH)

    @pl.loop(1, n_lon)
    def _(d):
        pl.semaphore_signal(barrier, inc=1, device_id={"lon": lax.rem(lon + d, n_lon)}, device_id_type=MESH)

    has_south = lat > 0
    has_north = lat < n_lat - 1

    def halo_f(i, v):
        return (
            (None, remote(v.at[rows(1)], recv_f.at[i, 0], hf_send.at[i, 0], hf_recv.at[i, 0], {"lon": east})),
            (None, remote(v.at[rows(0)], recv_f.at[i, 1], hf_send.at[i, 1], hf_recv.at[i, 1], {"lon": west})),
            (has_north, remote(v.at[rows(3)], recv_f.at[i, 2], hf_send.at[i, 2], hf_recv.at[i, 2], {"lat": lat + 1})),
            (has_south, remote(v.at[rows(2)], recv_f.at[i, 3], hf_send.at[i, 3], hf_recv.at[i, 3], {"lat": lat - 1})),
        )

    def halo_s(i):
        return (
            (None, remote(sp.at[i, 0], recv_s.at[i, 1], hs_send.at[i, 0], hs_recv.at[i, 1], {"lon": west})),
            (None, remote(sp.at[i, 1], recv_s.at[i, 0], hs_send.at[i, 1], hs_recv.at[i, 0], {"lon": east})),
            (has_south, remote(sp.at[i, 2], recv_s.at[i, 3], hs_send.at[i, 2], hs_recv.at[i, 3], {"lat": lat - 1})),
            (has_north, remote(sp.at[i, 3], recv_s.at[i, 2], hs_send.at[i, 3], hs_recv.at[i, 2], {"lat": lat + 1})),
        )

    def on(condition, action):
        if condition is None:
            action()
        else:
            pl.when(condition)(action)

    def start(copies):
        for condition, copy in copies:
            on(condition, copy.start)

    def sent(copies):
        for condition, copy in copies:
            on(condition, copy.wait_send)

    def landed(i, buffer, sems):
        for j, condition in ((0, None), (1, None), (2, has_south), (3, has_north)):
            at = buffer.at[i, j]
            on(condition, remote(at, at, hf_send.at[i, j], sems.at[i, j], {"lon": east}).wait_recv)

    def put_s(k, t, value):
        s[k, rows(t), :] = value
        hi, lo = split(value)
        s_hl[k, rows(t), 0:128] = hi
        s_hl[k, rows(t), 128:256] = lo

    def spread(i):
        for t in range(TILES):
            a = s_hl[i, rows(t), :]
            low = jnp.concatenate([a[:, 0:128], jnp.zeros((128, 128), BF16)], axis=1)
            r = dot(bt[t], jnp.concatenate([a, low], axis=0))
            share = r[:, 0:128] + r[:, 128:256]
            loc[t] = share[0:128]
            if t < 4:
                loc[6 + t] = share[128:256]
            else:
                free[2 + t] = share[128:256]
            free[t] = share[256:384]

        def gathered(e):
            total = loc[e]
            for f in range(8):
                entry = src[f, 2] if f < 6 else src[f - 2, 1]
                total = total + (entry == e).astype(F32) * free[f]
            return total

        @pl.loop(6, 10)
        def _(e):
            sp[i, e - 6] = gathered(e)

        start(halo_s(i))

        @pl.loop(0, 6)
        def _(e):
            loc[e] = gathered(e)

    def finish_s(i):
        landed(i, recv_s, hs_recv)
        for t in range(TILES):
            total = loc[t]
            if t < 4:
                total = total + recv_s[i, t]
            total = total * mask(t)
            if i > 0:
                total = 2.0 * total - s[i - 1, rows(t), :]
            put_s(i + 1, t, total)

    def put_ext(t, value):
        hi, lo = split(value)
        ext[t, :, 0:128] = hi
        ext[t, :, 128:256] = lo

    def apply(t):
        x = jnp.concatenate([ext[src[t, 0]], ext[src[t, 1]], ext[src[t, 2]]], axis=0)
        r = dot(bb[t], x)
        return (r[0:128, 0:128] + (r[0:128, 128:256] + r[128:256, 0:128])) * mask(t)

    def halo_in(i):
        landed(i, recv_f, hf_recv)
        for j in range(4):
            put_ext(6 + j, recv_f[i, j])

    def wg_partial(k):
        a = s_hl[k]
        r = dot(ft_hi[...], a)
        r = (r[:, 0:128] + r[:, 128:256] + dot(ft_lo[...], a[:, 0:128])) * scale
        wg_part[k, mine, :] = r[0:128]
        wg_part[k, other, :] = r[128:256]
        for d in range(1, n_lat):
            x_copy(k, d).start()

    def part_of(index):
        return pl.ds(pl.multiple_of(index * part, 8), part)

    def piece_of(index):
        return pl.ds(pl.multiple_of(index * piece, 8), piece)

    def x_copy(k, d):
        to = lax.rem(lat + d, n_lat)
        return remote(wg_part.at[k, part_of(to)], rx.at[k, d - 1], rx_send.at[k, d - 1], rx_recv.at[k, d - 1], {"lat": to})

    def z_copy(k, d):
        to = lax.rem(lon + d, n_lon)
        return to, remote(wg_x.at[k, piece_of(to)], rz.at[k, d - 1], rz_send.at[k, d - 1], rz_recv.at[k, d - 1], {"lon": to})

    def final_piece(k, owner):
        return wg_sum.at[k, pl.ds(pl.multiple_of(lat * part + owner * piece, 8), piece)]

    def az_copy(k, d):
        at = final_piece(k, lon)
        return remote(at, at, az_send.at[k, d - 1], az_recv.at[k, d - 1], {"lon": lax.rem(lon + d, n_lon)})

    def ax_copy(k, d):
        at = wg_sum.at[k, part_of(lat)]
        return remote(at, at, ax_send.at[k, d - 1], ax_recv.at[k, d - 1], {"lat": lax.rem(lat + d, n_lat)})

    def each_lon(body):
        if n_lon <= 4:
            for d in range(1, n_lon):
                body(d)
        else:
            pl.loop(1, n_lon)(body)

    everyone = own_lon == n_lon
    is_owner = None if everyone else lon < own_lon

    def owner_only(index, action):
        on(None if everyone else index < own_lon, action)

    def wg_lat(k):
        total = wg_part[k, part_of(lat), :]
        for d in range(1, n_lat):
            x_copy(k, d).wait_recv()
            total = total + rx[k, d - 1]
        wg_x[k] = total

        def send(d):
            to, copy = z_copy(k, d)
            owner_only(to, copy.start)

        each_lon(send)

    def wg_lon(k):
        def total_up():
            each_lon(lambda d: z_copy(k, d)[1].wait_recv())
            total = wg_x[k, piece_of(lon), :]
            if n_lon <= 4:
                for d in range(1, n_lon):
                    total = total + rz[k, d - 1]
            else:
                total = lax.fori_loop(1, n_lon, lambda d, t: t + rz[k, d - 1], total)
            wg_sum[k, pl.ds(pl.multiple_of(lat * part + lon * piece, 8), piece), :] = total
            each_lon(lambda d: az_copy(k, d).start())

        on(is_owner, total_up)

    def wg_back(k):
        def take(d):
            owner = lax.rem(lon + n_lon - d, n_lon)

            def wait():
                at = final_piece(k, owner)
                remote(at, at, az_send.at[k, d - 1], az_recv.at[k, d - 1], {"lon": east}).wait_recv()

            owner_only(owner, wait)

        each_lon(take)
        for d in range(1, n_lat):
            ax_copy(k, d).start()

    def wg_done(k):
        for d in range(1, n_lat):
            at = wg_sum.at[k, part_of(lax.rem(lat + n_lat - d, n_lat))]
            remote(at, at, ax_send.at[k, d - 1], ax_recv.at[k, d - 1], {"lon": east}).wait_recv()
        wg[k] = wg_sum[k]

    def wg_sent(k):
        for d in range(1, n_lat):
            x_copy(k, d).wait_send()
            ax_copy(k, d).wait_send()

        def wait(d):
            to, copy = z_copy(k, d)
            owner_only(to, copy.wait_send)

        each_lon(wait)
        on(is_owner, lambda: each_lon(lambda d: az_copy(k, d).wait_send()))

    def ig_copy(i):
        return remote(ig_send.at[i], ig_recv.at[i], ig_ssem.at[i], ig_rsem.at[i], {"ch": 1 - ch})

    def ig_term(k, t):
        a = s_hl[k, rows(t), :]
        return dot(a, wt_hh[k]) + dot(a[:, 0:128], wt_lo[k])

    for t in range(TILES):
        for j in range(3):
            hi, lo = split(blocks[t, j].T)
            bt[t, j * 128:(j + 1) * 128, 0:128] = hi
            bt[t, j * 128:(j + 1) * 128, 128:256] = lo
        put_s(0, t, cot[rows(t), :] * mask(t))

    @pl.when(jnp.logical_not(has_south))
    def _():
        for i in range(3):
            recv_f[i, 2] = jnp.zeros((128, 128), F32)
            recv_s[i, 2] = jnp.zeros((128, 128), F32)

    @pl.when(jnp.logical_not(has_north))
    def _():
        for i in range(3):
            recv_f[i, 3] = jnp.zeros((128, 128), F32)
            recv_s[i, 3] = jnp.zeros((128, 128), F32)

    pl.semaphore_wait(barrier, (n_lat - 1) + (n_lon - 1) + 1)
    feat_copy = remote(feat, fx, fx_sem.at[0], fx_sem.at[1], {"ch": 1 - ch})
    feat_copy.start()
    spread(0)

    for k in range(CHEB):
        for half, at in ((0, mine), (1, other)):
            value = w[k, at, :]
            hi, lo = split(value)
            w_hl[k, half * 128:(half + 1) * 128, 0:128] = hi
            w_hl[k, half * 128:(half + 1) * 128, 128:256] = lo
            hi, lo = split(value.T)
            wt_hh[k, 0:128, half * 128:(half + 1) * 128] = hi
            wt_hh[k, 128:256, half * 128:(half + 1) * 128] = hi
            wt_lo[k, :, half * 128:(half + 1) * 128] = lo

    feat_copy.wait_recv()
    for t in range(TILES):
        for half, ref in ((0, feat), (1, fx)):
            value = ref[rows(t), :] * mask(t)
            hi, lo = split(value)
            f_hi[rows(t), half * 128:(half + 1) * 128] = hi
            f_lo[rows(t), half * 128:(half + 1) * 128] = lo

    def mixed(k):
        for t in range(0, ROWS, 256):
            at = pl.ds(t, 256)
            r = dot(f_hi[at, :], w_hl[k])
            u[k, at, :] = r[:, 0:128] + r[:, 128:256] + dot(f_lo[at, :], w_hl[k, :, 0:128])

    mixed(3)
    start(halo_f(0, u.at[3]))
    for t in range(TILES):
        for j in range(3):
            hi, lo = split(blocks[t, j])
            bb[t, 0:128, j * 128:(j + 1) * 128] = hi
            bb[t, 128:256, j * 128:(j + 1) * 128] = lo
    for t in range(TILES):
        put_ext(t, u[3, rows(t), :])
        for half, ref in ((0, feat), (1, fx)):
            hi, lo = split((ref[rows(t), :] * mask(t)).T)
            ft_hi[half * 128:(half + 1) * 128, t * 128:(t + 1) * 128] = hi
            ft_lo[half * 128:(half + 1) * 128, t * 128:(t + 1) * 128] = lo

    finish_s(0)
    spread(1)
    wg_partial(0)
    mixed(2)

    halo_in(0)
    for t in range(TILES):
        b[0, rows(t), :] = u[2, rows(t), :] + 2.0 * apply(t)
    start(halo_f(1, b.at[0]))
    for t in range(TILES):
        put_ext(t, b[0, rows(t), :])
    wg_partial(1)
    wg_lat(0)
    mixed(1)

    finish_s(1)
    spread(2)
    wg_lat(1)
    wg_lon(0)
    wg_partial(2)

    halo_in(1)
    for t in range(TILES):
        b[1, rows(t), :] = u[1, rows(t), :] + 2.0 * apply(t) - u[3, rows(t), :]
    start(halo_f(2, b.at[1]))
    for t in range(TILES):
        put_ext(t, b[1, rows(t), :])
    for t in range(TILES):
        r = ig_term(0, t) + ig_term(1, t) + ig_term(2, t)
        ig_acc[rows(t), :] = r[:, 0:128]
        ig_send[0, rows(t), :] = r[:, 128:256]
    ig_copy(0).start()
    wg_lon(1)
    wg_lat(2)
    wg_back(0)

    finish_s(2)
    wg_partial(3)
    for t in range(TILES):
        r = ig_term(3, t)
        ig_acc[rows(t), :] += r[:, 0:128]
        ig_send[1, rows(t), :] = r[:, 128:256]
    ig_copy(1).start()
    wg_lon(2)
    wg_back(1)
    mixed(0)
    wg_lat(3)

    halo_in(2)
    for t in range(TILES):
        out[rows(t), :] = u[0, rows(t), :] + apply(t) - b[0, rows(t), :]
    wg_lon(3)
    wg_back(2)
    ig_copy(0).wait_recv()
    ig_copy(1).wait_recv()
    for t in range(TILES):
        at = rows(t)
        ig[at, :] = (ig_acc[at, :] + (ig_recv[0, at, :] + ig_recv[1, at, :])) * mask(t)
    wg_back(3)
    for k in range(CHEB):
        wg_done(k)

    feat_copy.wait_send()
    for i in range(3):
        sent(halo_f(i, (u.at[3], b.at[0], b.at[1])[i]))
        sent(halo_s(i))
    ig_copy(0).wait_send()
    ig_copy(1).wait_send()
    for k in range(CHEB):
        wg_sent(k)


def shards(n_lon, n_lat, features, blocks, sources, live, weights, cotangent):
    own_lon = min(n_lon, 256 // n_lat // 8)
    part = 256 // n_lat
    piece = part // own_lon
    scale = float(ROWS * n_lon * n_lat) ** (-0.5)
    vmem = pl.BlockSpec(memory_space=pltpu.VMEM)
    smem = pl.BlockSpec(memory_space=pltpu.SMEM)
    dma = pltpu.SemaphoreType.DMA
    lons, lats = max(n_lon - 1, 1), max(n_lat - 1, 1)
    return pl.pallas_call(
        functools.partial(kernel, n_lon, n_lat, own_lon, scale),
        out_shape=(
            jax.ShapeDtypeStruct((ROWS, 128), F32),
            jax.ShapeDtypeStruct((ROWS, 128), F32),
            jax.ShapeDtypeStruct((CHEB, 256, 128), F32),
        ),
        in_specs=[vmem, vmem, smem, smem, vmem, vmem],
        out_specs=(vmem, vmem, vmem),
        scratch_shapes=[
            pltpu.VMEM((ROWS, 128), F32),
            pltpu.VMEM((ROWS, 256), BF16),
            pltpu.VMEM((ROWS, 256), BF16),
            pltpu.VMEM((256, ROWS), BF16),
            pltpu.VMEM((256, ROWS), BF16),
            pltpu.VMEM((CHEB, 256, 256), BF16),
            pltpu.VMEM((CHEB, 256, 256), BF16),
            pltpu.VMEM((CHEB, 128, 256), BF16),
            pltpu.VMEM((TILES, 256, 384), BF16),
            pltpu.VMEM((TILES, 384, 256), BF16),
            pltpu.VMEM((CHEB, ROWS, 128), F32),
            pltpu.VMEM((2, ROWS, 128), F32),
            pltpu.VMEM((CHEB, ROWS, 128), F32),
            pltpu.VMEM((CHEB, ROWS, 256), BF16),
            pltpu.VMEM((TILES + 4, 128, 256), BF16),
            pltpu.VMEM((TILES + 4, 128, 128), F32),
            pltpu.VMEM((8, 128, 128), F32),
            pltpu.VMEM((3, 4, 128, 128), F32),
            pltpu.VMEM((3, 4, 128, 128), F32),
            pltpu.VMEM((3, 4, 128, 128), F32),
            pltpu.VMEM((ROWS, 128), F32),
            pltpu.VMEM((2, ROWS, 128), F32),
            pltpu.VMEM((2, ROWS, 128), F32),
            pltpu.VMEM((CHEB, 256, 128), F32),
            pltpu.VMEM((CHEB, lats, part, 128), F32),
            pltpu.VMEM((CHEB, part, 128), F32),
            pltpu.VMEM((CHEB, lons, piece, 128), F32),
            pltpu.VMEM((CHEB, 256, 128), F32),
            dma((2,)),
            dma((3, 4)), dma((3, 4)),
            dma((3, 4)), dma((3, 4)),
            dma((2,)), dma((2,)),
            dma((CHEB, lats)), dma((CHEB, lats)),
            dma((CHEB, lons)), dma((CHEB, lons)),
            dma((CHEB, lons)), dma((CHEB, lons)),
            dma((CHEB, lats)), dma((CHEB, lats)),
        ],
        compiler_params=pltpu.CompilerParams(
            collective_id=0, has_side_effects=True, vmem_limit_bytes=48 * 1024 * 1024
        ),
        cost_estimate=pl.CostEstimate(flops=3_200_000_000, bytes_accessed=4_200_000, transcendentals=0),
    )(features, blocks, sources, live, weights, cotangent)


def solution(mesh):
    placed = (
        P(("groups", "lon", "lat"), "ch"),
        P(("lon", "lat"), None, None, None),
        P(("lon", "lat"), None),
        P(("lon", "lat")),
        P(None, None, "ch"),
        P(("groups", "lon", "lat"), "ch"),
    )
    return jax.shard_map(
        functools.partial(shards, mesh.shape["lon"], mesh.shape["lat"]),
        mesh=mesh,
        in_specs=placed,
        out_specs=(
            P(("groups", "lon", "lat"), "ch"),
            P(("groups", "lon", "lat"), "ch"),
            P("groups", None, "ch"),
        ),
        check_vma=False,
    )
```

time: 201 us -> 53.8 us (0.27)
  starting transfers between devices: 56 us -> 0 us
  Pallas kernels: 0 us -> 44.8 us
  matrix products: 43.8 us -> 0 us
  waiting for transfers between devices: 34.4 us -> 0 us
  local copies, waits for them, and re-layouts: 35.4 us -> 7.36 us
  between operations: 16.9 us -> 1.29 us
  blocking collectives: 9.94 us -> 0 us
  other arithmetic: 3.38 us -> 0 us
    ppermute x24 -> x0, starting transfers between devices: 56 us -> none  [the longest x12 28.9 us: padded(): after = lax.ppermute(leading, axis, down)]
    pallas_call x0 -> x1, Pallas kernels: none -> 44.8 us  [shards(): pl.pallas_call(functools.partial(kernel, n_lon, n_lat, own_lon, scale), o...]
    dot_general x18 -> x0, matrix products: 43.8 us -> none  [the longest x3 9.78 us: adjoint_apply(): jnp.einsum('yerj,yri->yeji', blocks, pixel_field * keep_mask, precision=h...]
    psum x1 -> x0, waiting for transfers between devices: 27.3 us -> none  [shards(): weight_grad = lax.psum(weight_grad, ('lon', 'lat'))]
    all_gather x4 -> x0, blocking collectives: 9.94 us -> none  [mix_split(): piece = lax.all_gather(term, 'ch', axis=2, tiled=True)]
    gather x6 -> x0, local copies, waits for them, and re-layouts: 9.73 us -> none  [forward_apply(): selected_entries = jnp.take(extended, sources, axis=0)]
    slice x14 -> x0, local copies, waits for them, and re-layouts: 8.31 us -> none  [the longest x5 5.46 us: adjoint_apply(): return jnp.concatenate([local[:4] + edges, local[4:]], axis=0) * keep_mask]
    ppermute x24 -> x0, waiting for transfers between devices: 7.04 us -> none  [the longest x12 5.29 us: padded(): after = lax.ppermute(leading, axis, down)]
  transfers between devices with their start and end apart: 26 -> 0, of which waited for: 7 -> 0; matrix products, arithmetic and copies ran while one was open for 32% -> 0% of each run, Pallas kernels for 0% -> 0%
where the time goes in v1:
time: 53.8 us; the launch traced here: 53.5 us
  Pallas kernels  44.8 us (83%)
  local copies, waits for them, and re-layouts  7.36 us (14%)
  between operations  1.29 us (2%)
    pallas_call x1, Pallas kernels, shards(): pl.pallas_call(functools.partial(kernel, n_lon, n_lat, own_lon, scale), o...  44.8 us
    unnamed x12, local copies, waits for them, and re-layouts  7.36 us

profile of v1, /device:TPU:0, one launch (start us, length us, event | category | flops | bytes accessed | tf_op | source)
XLA Modules:
  0.0 53.5 jit_solution(1427982773778323570)
XLA Ops:
  1.3 0.8 %copy.9.src = s32[6,3]{1,0:T(8,128)S(1)} copy(s32[6,3]{0,1:T(4,128)} %param.8) | data formatting | bytes 144 | tf_op args[2]
  2.0 0.0 copy-start
  2.0 1.3 %copy-done = f32[6,3,128,128]{3,2,1,0:T(8,128)S(1)} copy-done((f32[6,3,128,128]{3,2,1,0:T(8,128)S(1)}, f32[6,3,128,128]{3,2,1,0:T(8,128)}, u32[]{:S(2)}) %copy-start) | copy-done | bytes 1179672
  3.3 0.0 copy-start.1
  3.3 1.0 %copy-done.1 = f32[4,256,128]{2,1,0:T(8,128)S(1)} copy-done((f32[4,256,128]{2,1,0:T(8,128)S(1)}, f32[4,256,128]{2,1,0:T(8,128)}, u32[]{:S(2)}) %copy-start.1) | copy-done | bytes 524312
  4.4 0.0 copy-start.2
  4.4 1.0 %copy-done.2 = f32[768,128]{1,0:T(8,128)S(1)} copy-done((f32[768,128]{1,0:T(8,128)S(1)}, f32[768,128]{1,0:T(8,128)}, u32[]{:S(2)}) %copy-start.2) | copy-done | bytes 393240
  5.4 0.0 copy-start.3
  5.4 1.0 %copy-done.3 = f32[768,128]{1,0:T(8,128)S(1)} copy-done((f32[768,128]{1,0:T(8,128)S(1)}, f32[768,128]{1,0:T(8,128)}, u32[]{:S(2)}) %copy-start.3) | copy-done | bytes 393240
  6.4 44.8 %shard_map.85 = (f32[768,128]{1,0:T(8,128)S(1)}, f32[768,128]{1,0:T(8,128)S(1)}, f32[4,256,128]{2,1,0:T(8,128)S(1)}) custom-call(f32[768,128]{1,0:T(8,128)S(1)} %copy-done.2, f32[6,3,128,128]{3,2,1,0:T(8,128)S(1)} %copy-done, s32[6,3]{1,0:T(8,128)S(1)} %copy.9.src, s32[1]{0:T(128)S(6)} %copy.13.live, f32[4,256,128]{2,1,0:T(8,128)S(1)} %copy-done.1, ...), custom_call_target="tpu_custom_call" | custom-call | flops 3200000000 | bytes 4200000 | tf_op jit(solution)/shard_map/pallas_call | solution.py:426
  51.2 0.7 %copy.14 = f32[768,128]{1,0:T(8,128)} copy(f32[768,128]{1,0:T(8,128)S(1)} %get-tuple-element.6) | data formatting | bytes 786432
  51.9 0.7 %copy.15 = f32[768,128]{1,0:T(8,128)} copy(f32[768,128]{1,0:T(8,128)S(1)} %get-tuple-element.7) | data formatting | bytes 786432
  52.7 0.8 %copy.16 = f32[4,256,128]{2,1,0:T(8,128)} copy(f32[4,256,128]{2,1,0:T(8,128)S(1)} %get-tuple-element.8) | data formatting | bytes 1048576
Async XLA Ops:
  2.0 1.3 %copy-start = (f32[6,3,128,128]{3,2,1,0:T(8,128)S(1)}, f32[6,3,128,128]{3,2,1,0:T(8,128)}, u32[]{:S(2)}) copy-start(f32[6,3,128,128]{3,2,1,0:T(8,128)} %blocks.1) | copy-start | bytes 3538948
  3.3 1.0 %copy-start.1 = (f32[4,256,128]{2,1,0:T(8,128)S(1)}, f32[4,256,128]{2,1,0:T(8,128)}, u32[]{:S(2)}) copy-start(f32[4,256,128]{2,1,0:T(8,128)} %w.1) | copy-start | bytes 1572868
  4.4 1.0 %copy-start.2 = (f32[768,128]{1,0:T(8,128)S(1)}, f32[768,128]{1,0:T(8,128)}, u32[]{:S(2)}) copy-start(f32[768,128]{1,0:T(8,128)} %feat.1) | copy-start | bytes 1179652
  5.4 1.0 %copy-start.3 = (f32[768,128]{1,0:T(8,128)S(1)}, f32[768,128]{1,0:T(8,128)}, u32[]{:S(2)}) copy-start(f32[768,128]{1,0:T(8,128)} %cot.1) | copy-start | bytes 1179652

commit v2 on v1

--- a/solution.py
+++ b/solution.py
@@ -27,13 +27,14 @@
 
 def kernel(
     n_lon, n_lat, own_lon, scale,
-    feat, blocks, src, live, w, cot,
+    feat_in, blocks_in, src, live, w_in, cot_in,
     out, ig, wg,
-    fx, f_hi, f_lo, ft_hi, ft_lo, w_hl, wt_hh, wt_lo, bb, bt,
-    u, b, s, s_hl, ext, loc, free, sp,
+    feat, blocks, w, cot, in_sem,
+    tx, t_hl, ft_hi, ft_lo, w_hl, wt_hh, wt_lo, bb, bt,
+    term, mix, s, s_hl, ext, loc, free, sp,
     recv_f, recv_s, ig_acc, ig_send, ig_recv,
     wg_part, rx, wg_x, rz, wg_sum,
-    fx_sem, hf_send, hf_recv, hs_send, hs_recv, ig_ssem, ig_rsem,
+    tx_send, tx_recv, hf_send, hf_recv, hs_send, hs_recv, ig_ssem, ig_rsem,
     rx_send, rx_recv, rz_send, rz_recv, az_send, az_recv, ax_send, ax_recv,
 ):
     part = 256 // n_lat
@@ -56,6 +57,13 @@
         return pltpu.make_async_remote_copy(
             src_ref=a, dst_ref=d, send_sem=ssem, recv_sem=rsem, device_id=dev, device_id_type=MESH
         )
+
+    inputs = [
+        pltpu.make_async_copy(a, d, in_sem.at[i])
+        for i, (a, d) in enumerate(((blocks_in, blocks), (cot_in, cot), (w_in, w), (feat_in, feat)))
+    ]
+    for copy in inputs:
+        copy.start()
 
     barrier = pltpu.get_barrier_semaphore()
     pl.semaphore_signal(barrier, inc=1, device_id={"ch": 1 - ch}, device_id_type=MESH)
@@ -126,7 +134,7 @@
         def gathered(e):
             total = loc[e]
             for f in range(8):
-                entry = src[f, 2] if f < 6 else src[f - 2, 1]
+                entry = src[2, f] if f < 6 else src[1, f - 2]
                 total = total + (entry == e).astype(F32) * free[f]
             return total
 
@@ -156,8 +164,47 @@
         ext[t, :, 0:128] = hi
         ext[t, :, 128:256] = lo
 
+    def put_split(k, t):
+        hi, lo = split(term[k, rows(t), :])
+        t_hl[k, 0, rows(t), 0:128] = hi
+        t_hl[k, 1, rows(t), 0:128] = lo
+        if k < CHEB - 1:
+            ext[t, :, 0:128] = hi
+            ext[t, :, 128:256] = lo
+
+    def term_copy(k):
+        a = feat_in if k == 0 else term.at[k]
+        return remote(a, tx.at[k], tx_send.at[k], tx_recv.at[k], {"ch": 1 - ch})
+
+    def term_in(k):
+        term_copy(k).wait_recv()
+        for t in range(TILES):
+            value = tx[k, rows(t), :]
+            if k == 0:
+                value = value * mask(t)
+            hi, lo = split(value)
+            t_hl[k, 0, rows(t), 128:256] = hi
+            t_hl[k, 1, rows(t), 128:256] = lo
+            if k < 2:
+                for side, x in ((0, term[k, rows(t), :]), (1, value)):
+                    hi, lo = split(x.T)
+                    ft_hi[k, side * 128:(side + 1) * 128, t * 128:(t + 1) * 128] = hi
+                    ft_lo[k, side * 128:(side + 1) * 128, t * 128:(t + 1) * 128] = lo
+
+    def mixed(k):
+        for t in range(0, ROWS, 256):
+            at = pl.ds(t, 256)
+            r = dot(t_hl[k, 0, at, :], w_hl[k])
+            r = r[:, 0:128] + r[:, 128:256] + dot(t_hl[k, 1, at, :], w_hl[k, :, 0:128])
+            if k == CHEB - 1:
+                out[at, :] = mix[at, :] + r
+            elif k == 0:
+                mix[at, :] = r
+            else:
+                mix[at, :] += r
+
     def apply(t):
-        x = jnp.concatenate([ext[src[t, 0]], ext[src[t, 1]], ext[src[t, 2]]], axis=0)
+        x = jnp.concatenate([ext[src[0, t]], ext[src[1, t]], ext[src[2, t]]], axis=0)
         r = dot(bb[t], x)
         return (r[0:128, 0:128] + (r[0:128, 128:256] + r[128:256, 0:128])) * mask(t)
 
@@ -166,12 +213,29 @@
         for j in range(4):
             put_ext(6 + j, recv_f[i, j])
 
+    def next_term(i):
+        halo_in(i)
+        for t in range(TILES):
+            total = apply(t)
+            if i > 0:
+                total = 2.0 * total - term[i - 1, rows(t), :]
+            term[i + 1, rows(t), :] = total
+        if i < 2:
+            start(halo_f(i + 1, term.at[i + 1]))
+        term_copy(i + 1).start()
+        for t in range(TILES):
+            put_split(i + 1, t)
+
     def wg_partial(k):
-        a = s_hl[k]
-        r = dot(ft_hi[...], a)
-        r = (r[:, 0:128] + r[:, 128:256] + dot(ft_lo[...], a[:, 0:128])) * scale
-        wg_part[k, mine, :] = r[0:128]
-        wg_part[k, other, :] = r[128:256]
+        first, second = (0, k) if k < 2 else (1, k - 1)
+        a = s_hl[second]
+        r = dot(ft_hi[first], a)
+        r = (r[:, 0:128] + r[:, 128:256] + dot(ft_lo[first], a[:, 0:128])) * scale
+        for half, at in ((0, mine), (1, other)):
+            value = r[half * 128:(half + 1) * 128]
+            if k >= 2:
+                value = 2.0 * value - wg_part[k - 2, at, :]
+            wg_part[k, at, :] = value
         for d in range(1, n_lat):
             x_copy(k, d).start()
 
@@ -279,139 +343,125 @@
         a = s_hl[k, rows(t), :]
         return dot(a, wt_hh[k]) + dot(a[:, 0:128], wt_lo[k])
 
+    @pl.when(jnp.logical_not(has_south))
+    def _():
+        for i in range(3):
+            recv_f[i, 2] = jnp.zeros((128, 128), F32)
+            recv_s[i, 2] = jnp.zeros((128, 128), F32)
+
+    @pl.when(jnp.logical_not(has_north))
+    def _():
+        for i in range(3):
+            recv_f[i, 3] = jnp.zeros((128, 128), F32)
+            recv_s[i, 3] = jnp.zeros((128, 128), F32)
+
+    pl.semaphore_wait(barrier, (n_lat - 1) + (n_lon - 1) + 1)
+    start(halo_f(0, feat_in))
+    term_copy(0).start()
+
+    inputs[0].wait()
+    inputs[1].wait()
     for t in range(TILES):
         for j in range(3):
             hi, lo = split(blocks[t, j].T)
             bt[t, j * 128:(j + 1) * 128, 0:128] = hi
             bt[t, j * 128:(j + 1) * 128, 128:256] = lo
         put_s(0, t, cot[rows(t), :] * mask(t))
-
-    @pl.when(jnp.logical_not(has_south))
-    def _():
-        for i in range(3):
-            recv_f[i, 2] = jnp.zeros((128, 128), F32)
-            recv_s[i, 2] = jnp.zeros((128, 128), F32)
-
-    @pl.when(jnp.logical_not(has_north))
-    def _():
-        for i in range(3):
-            recv_f[i, 3] = jnp.zeros((128, 128), F32)
-            recv_s[i, 3] = jnp.zeros((128, 128), F32)
-
-    pl.semaphore_wait(barrier, (n_lat - 1) + (n_lon - 1) + 1)
-    feat_copy = remote(feat, fx, fx_sem.at[0], fx_sem.at[1], {"ch": 1 - ch})
-    feat_copy.start()
     spread(0)
 
-    for k in range(CHEB):
-        for half, at in ((0, mine), (1, other)):
-            value = w[k, at, :]
-            hi, lo = split(value)
-            w_hl[k, half * 128:(half + 1) * 128, 0:128] = hi
-            w_hl[k, half * 128:(half + 1) * 128, 128:256] = lo
-            hi, lo = split(value.T)
-            wt_hh[k, 0:128, half * 128:(half + 1) * 128] = hi
-            wt_hh[k, 128:256, half * 128:(half + 1) * 128] = hi
-            wt_lo[k, :, half * 128:(half + 1) * 128] = lo
-
-    feat_copy.wait_recv()
-    for t in range(TILES):
-        for half, ref in ((0, feat), (1, fx)):
-            value = ref[rows(t), :] * mask(t)
-            hi, lo = split(value)
-            f_hi[rows(t), half * 128:(half + 1) * 128] = hi
-            f_lo[rows(t), half * 128:(half + 1) * 128] = lo
-
-    def mixed(k):
-        for t in range(0, ROWS, 256):
-            at = pl.ds(t, 256)
-            r = dot(f_hi[at, :], w_hl[k])
-            u[k, at, :] = r[:, 0:128] + r[:, 128:256] + dot(f_lo[at, :], w_hl[k, :, 0:128])
-
-    mixed(3)
-    start(halo_f(0, u.at[3]))
+    inputs[2].wait()
+    inputs[3].wait()
     for t in range(TILES):
         for j in range(3):
             hi, lo = split(blocks[t, j])
             bb[t, 0:128, j * 128:(j + 1) * 128] = hi
             bb[t, 128:256, j * 128:(j + 1) * 128] = lo
-    for t in range(TILES):
-        put_ext(t, u[3, rows(t), :])
-        for half, ref in ((0, feat), (1, fx)):
-            hi, lo = split((ref[rows(t), :] * mask(t)).T)
-            ft_hi[half * 128:(half + 1) * 128, t * 128:(t + 1) * 128] = hi
-            ft_lo[half * 128:(half + 1) * 128, t * 128:(t + 1) * 128] = lo
+        term[0, rows(t), :] = feat[rows(t), :] * mask(t)
+        put_split(0, t)
+
+    next_term(0)
+    term_in(0)
+    wg_partial(0)
 
     finish_s(0)
     spread(1)
-    wg_partial(0)
-    mixed(2)
-
-    halo_in(0)
-    for t in range(TILES):
-        b[0, rows(t), :] = u[2, rows(t), :] + 2.0 * apply(t)
-    start(halo_f(1, b.at[0]))
-    for t in range(TILES):
-        put_ext(t, b[0, rows(t), :])
     wg_partial(1)
+    term_in(1)
+    wg_partial(2)
     wg_lat(0)
+    for k in range(CHEB):
+        for side, at in ((0, mine), (1, other)):
+            value = w[k, at, :]
+            hi, lo = split(value)
+            w_hl[k, side * 128:(side + 1) * 128, 0:128] = hi
+            w_hl[k, side * 128:(side + 1) * 128, 128:256] = lo
+            hi, lo = split(value.T)
+            wt_hh[k, 0:128, side * 128:(side + 1) * 128] = hi
+            wt_hh[k, 128:256, side * 128:(side + 1) * 128] = hi
+            wt_lo[k, :, side * 128:(side + 1) * 128] = lo
+
+    next_term(1)
+    wg_lat(1)
+    wg_lat(2)
+    wg_lon(0)
+    mixed(0)
     mixed(1)
 
     finish_s(1)
     spread(2)
-    wg_lat(1)
-    wg_lon(0)
-    wg_partial(2)
-
-    halo_in(1)
-    for t in range(TILES):
-        b[1, rows(t), :] = u[1, rows(t), :] + 2.0 * apply(t) - u[3, rows(t), :]
-    start(halo_f(2, b.at[1]))
-    for t in range(TILES):
-        put_ext(t, b[1, rows(t), :])
+    wg_partial(3)
+    wg_lon(1)
+    wg_lon(2)
+    wg_back(0)
+    term_in(2)
+    mixed(2)
     for t in range(TILES):
         r = ig_term(0, t) + ig_term(1, t) + ig_term(2, t)
         ig_acc[rows(t), :] = r[:, 0:128]
         ig_send[0, rows(t), :] = r[:, 128:256]
     ig_copy(0).start()
-    wg_lon(1)
-    wg_lat(2)
-    wg_back(0)
+    wg_lat(3)
+
+    next_term(2)
+    wg_lon(3)
+    wg_back(1)
+    wg_back(2)
 
     finish_s(2)
-    wg_partial(3)
     for t in range(TILES):
         r = ig_term(3, t)
         ig_acc[rows(t), :] += r[:, 0:128]
         ig_send[1, rows(t), :] = r[:, 128:256]
     ig_copy(1).start()
-    wg_lon(2)
-    wg_back(1)
-    mixed(0)
-    wg_lat(3)
-
-    halo_in(2)
-    for t in range(TILES):
-        out[rows(t), :] = u[0, rows(t), :] + apply(t) - b[0, rows(t), :]
-    wg_lon(3)
-    wg_back(2)
+    wg_back(3)
+    term_in(3)
+    mixed(3)
     ig_copy(0).wait_recv()
     ig_copy(1).wait_recv()
     for t in range(TILES):
         at = rows(t)
         ig[at, :] = (ig_acc[at, :] + (ig_recv[0, at, :] + ig_recv[1, at, :])) * mask(t)
-    wg_back(3)
     for k in range(CHEB):
         wg_done(k)
 
-    feat_copy.wait_send()
     for i in range(3):
-        sent(halo_f(i, (u.at[3], b.at[0], b.at[1])[i]))
+        sent(halo_f(i, feat_in if i == 0 else term.at[i]))
         sent(halo_s(i))
     ig_copy(0).wait_send()
     ig_copy(1).wait_send()
     for k in range(CHEB):
+        term_copy(k).wait_send()
         wg_sent(k)
+
+
+def write_out(a, b, c, a_out, b_out, c_out, sem):
+    copies = [
+        pltpu.make_async_copy(x, y, sem.at[i]) for i, (x, y) in enumerate(((a, a_out), (b, b_out), (c, c_out)))
+    ]
+    for copy in copies:
+        copy.start()
+    for copy in copies:
+        copy.wait()
 
 
 def shards(n_lon, n_lat, features, blocks, sources, live, weights, cotangent):
@@ -423,28 +473,33 @@
     smem = pl.BlockSpec(memory_space=pltpu.SMEM)
     dma = pltpu.SemaphoreType.DMA
     lons, lats = max(n_lon - 1, 1), max(n_lat - 1, 1)
-    return pl.pallas_call(
+    hbm = pl.BlockSpec(memory_space=pltpu.HBM)
+    results = pl.pallas_call(
         functools.partial(kernel, n_lon, n_lat, own_lon, scale),
         out_shape=(
             jax.ShapeDtypeStruct((ROWS, 128), F32),
             jax.ShapeDtypeStruct((ROWS, 128), F32),
             jax.ShapeDtypeStruct((CHEB, 256, 128), F32),
         ),
-        in_specs=[vmem, vmem, smem, smem, vmem, vmem],
+        in_specs=[hbm, hbm, smem, smem, hbm, hbm],
         out_specs=(vmem, vmem, vmem),
         scratch_shapes=[
             pltpu.VMEM((ROWS, 128), F32),
-            pltpu.VMEM((ROWS, 256), BF16),
-            pltpu.VMEM((ROWS, 256), BF16),
-            pltpu.VMEM((256, ROWS), BF16),
-            pltpu.VMEM((256, ROWS), BF16),
+            pltpu.VMEM((TILES, 3, 128, 128), F32),
+            pltpu.VMEM((CHEB, 256, 128), F32),
+            pltpu.VMEM((ROWS, 128), F32),
+            dma((4,)),
+            pltpu.VMEM((CHEB, ROWS, 128), F32),
+            pltpu.VMEM((CHEB, 2, ROWS, 256), BF16),
+            pltpu.VMEM((2, 256, ROWS), BF16),
+            pltpu.VMEM((2, 256, ROWS), BF16),
             pltpu.VMEM((CHEB, 256, 256), BF16),
             pltpu.VMEM((CHEB, 256, 256), BF16),
             pltpu.VMEM((CHEB, 128, 256), BF16),
             pltpu.VMEM((TILES, 256, 384), BF16),
             pltpu.VMEM((TILES, 384, 256), BF16),
             pltpu.VMEM((CHEB, ROWS, 128), F32),
-            pltpu.VMEM((2, ROWS, 128), F32),
+            pltpu.VMEM((ROWS, 128), F32),
             pltpu.VMEM((CHEB, ROWS, 128), F32),
             pltpu.VMEM((CHEB, ROWS, 256), BF16),
             pltpu.VMEM((TILES + 4, 128, 256), BF16),
@@ -461,7 +516,7 @@
             pltpu.VMEM((CHEB, part, 128), F32),
             pltpu.VMEM((CHEB, lons, piece, 128), F32),
             pltpu.VMEM((CHEB, 256, 128), F32),
-            dma((2,)),
+            dma((CHEB,)), dma((CHEB,)),
             dma((3, 4)), dma((3, 4)),
             dma((3, 4)), dma((3, 4)),
             dma((2,)), dma((2,)),
@@ -471,10 +526,18 @@
             dma((CHEB, lats)), dma((CHEB, lats)),
         ],
         compiler_params=pltpu.CompilerParams(
-            collective_id=0, has_side_effects=True, vmem_limit_bytes=48 * 1024 * 1024
+            collective_id=0, has_side_effects=True, vmem_limit_bytes=60 * 1024 * 1024
         ),
         cost_estimate=pl.CostEstimate(flops=3_200_000_000, bytes_accessed=4_200_000, transcendentals=0),
-    )(features, blocks, sources, live, weights, cotangent)
+    )(features, blocks, sources.T, live, weights, cotangent)
+    return pl.pallas_call(
+        write_out,
+        out_shape=tuple(jax.ShapeDtypeStruct(a.shape, a.dtype) for a in results),
+        in_specs=[vmem] * 3,
+        out_specs=(hbm,) * 3,
+        scratch_shapes=[dma((3,))],
+        cost_estimate=pl.CostEstimate(flops=0, bytes_accessed=2_600_000, transcendentals=0),
+    )(*results)
 
 
 def solution(mesh):

time: 53.8 us -> 47.9 us (0.89)
  local copies, waits for them, and re-layouts: 7.36 us -> 0 us
  Pallas kernels: 44.8 us -> 46.4 us
    unnamed x12 -> x0, local copies, waits for them, and re-layouts: 7.36 us -> none
    pallas_call x0 -> x1, Pallas kernels: none -> 2.36 us  [shards(): pl.pallas_call(write_out, out_shape=tuple((jax.ShapeDtypeStruct(a.shape,...]
    pallas_call x1, Pallas kernels: 44.8 us -> 44.1 us  [shards(): pl.pallas_call(functools.partial(kernel, n_lon, n_lat, own_lon, scale), o...]
where the time goes in v2:
time: 47.9 us; the launch traced here: 47.7 us
  Pallas kernels  46.4 us (97%)
  between operations  1.29 us (3%)
    pallas_call x1, Pallas kernels, shards(): pl.pallas_call(functools.partial(kernel, n_lon, n_lat, own_lon, scale), o...  44.1 us
    pallas_call x1, Pallas kernels, shards(): pl.pallas_call(write_out, out_shape=tuple((jax.ShapeDtypeStruct(a.shape,...  2.36 us

profile of v2, /device:TPU:0, one launch (start us, length us, event | category | flops | bytes accessed | tf_op | source)
XLA Modules:
  0.0 47.7 jit_solution(10721543494133597638)
XLA Ops:
  1.3 44.1 %shard_map.85 = (f32[768,128]{1,0:T(8,128)}, f32[768,128]{1,0:T(8,128)}, f32[4,256,128]{2,1,0:T(8,128)}) custom-call(f32[768,128]{1,0:T(8,128)} %feat_in.1, f32[6,3,128,128]{3,2,1,0:T(8,128)} %blocks_in.1, s32[3,6]{1,0:T(4,128)} %bitcast.1, s32[1]{0:T(128)S(6)} %copy.9.live, f32[4,256,128]{2,1,0:T(8,128)} %w_in.1, f32[768,128]{1,0:T(8,128)} %cot_in.1), custom_call_target="tpu_custom_call" | custom-call | flops 3200000000 | bytes 4200000 | tf_op jit(solution)/shard_map/pallas_call | solution.py:477
  45.4 2.4 %shard_map.86 = (f32[768,128]{1,0:T(8,128)}, f32[768,128]{1,0:T(8,128)}, f32[4,256,128]{2,1,0:T(8,128)}) custom-call(f32[768,128]{1,0:T(8,128)} %get-tuple-element.6.a, f32[768,128]{1,0:T(8,128)} %get-tuple-element.7.b, f32[4,256,128]{2,1,0:T(8,128)} %get-tuple-element.8.c), custom_call_target="tpu_custom_call" | custom-call | bytes 2600000 | tf_op jit(solution)/shard_map/pallas_call | solution.py:533
